TPU v7x, 32 devices: a whole 2x2x4 slice. The times are simulated.
32 devices in a mesh: dp: 4 (over x, core), ctx: 2 (over y), tp: 4 (over z).
Axes of the slice: x: 2, y: 2, z: 4, core: 2. Of those that a mesh axis runs over, the one named last changes fastest.
Arguments:
- query_rows: bfloat16 [2048, 4096], P(('dp', 'ctx'), 'tp'), parts along dimension 0, may hold values from -6 to 6
- key_matrix: bfloat16 [2048, 512], P(('dp', 'ctx'), 'tp'), parts along dimension 0, may hold values from -6 to 6
- value_matrix: bfloat16 [2048, 512], P(('dp', 'ctx'), 'tp'), parts along dimension 0, may hold values from -6 to 6
- attn_out: bfloat16 [2048, 4096], P(('dp', 'ctx'), 'tp'), parts along dimension 0, may hold values from -6 to 6
- out_grad: bfloat16 [2048, 4096], P(('dp', 'ctx', 'tp')), parts along dimension 0, may hold values from -0.5 to 0.5
- log_sums: float32 [32, 2048], P('tp', ('dp', 'ctx')), parts along dimension 1, may hold values from 3 to 5
- block_mask: int32 [16, 4], P('dp'), parts along dimension 0, may hold values 0 or 1
Outputs:
- query_grad: bfloat16 [2048, 4096], P(('dp', 'ctx'), 'tp'), parts along dimension 0
- key_gradient: bfloat16 [2048, 512], P(('dp', 'ctx'), 'tp'), parts along dimension 0
- value_gradient: bfloat16 [2048, 512], P(('dp', 'ctx'), 'tp'), parts along dimension 0
There are 4 independent parts, one for each index of `dp`. A program takes and returns all parts, laid end to end along the dimension named above; each array names one. Nothing has to cross between parts.
Inputs may be any that keep to these rules, and one draw needn't show every extreme that they name: `block_mask`: entry [a, b] with b < a lets query block a see key block b; entries on and above the diagonal are never read.
All inputs are finite; a program needn't handle non-finite values.
Results may differ from a plain program's by a relative error of at most 0.0049.
Values may be sent and summed in bfloat16 or wider, within the bound.
A program may use at most 64 MiB of HBM per device.

v0:
```python
import math

import jax
import jax.numpy as jnp
from jax import lax
from jax.sharding import PartitionSpec as P

BLK = 128
HEAD_SIZE = 128


def from_behind(value, axis, steps):
    count = lax.axis_size(axis)
    pairs = [(source, (source + steps) % count) for source in range(count)]
    return lax.ppermute(value, axis, pairs)


def live_region(block_mask, query_start, tok_rows, key_start, key_count):
    block_table = lax.dynamic_slice(
        block_mask, (query_start // BLK, key_start // BLK), (tok_rows // BLK, key_count // BLK)
    )
    block_table = jnp.repeat(jnp.repeat(block_table, BLK, axis=0), BLK, axis=1)
    query_pos = query_start + jnp.arange(tok_rows, dtype=jnp.int32)
    key_pos = key_start + jnp.arange(key_count, dtype=jnp.int32)
    query_block = (query_pos // BLK)[:, None]
    key_block = (key_pos // BLK)[None, :]
    earlier = (key_block < query_block) & (block_table == 1)
    diagonal = (key_block == query_block) & (key_pos[None, :] <= query_pos[:, None])
    return earlier | diagonal


def contract(queries, out_grads, row_delta, log_sums, keys_part, values_part, live_mask):
    logit_scale = 1.0 / math.sqrt(HEAD_SIZE)
    scores = (
        jnp.einsum("igd,jd->gij", queries, keys_part, preferred_element_type=jnp.float32)
        * logit_scale
    )
    probabilities = jnp.where(live_mask[None], jnp.exp(scores - log_sums[:, :, None]), 0.0)
    prob_grad = jnp.einsum(
        "igd,jd->gij", out_grads, values_part, preferred_element_type=jnp.float32
    )
    dscore = (probabilities * (prob_grad - row_delta[:, :, None])).astype(jnp.bfloat16)
    query_term = jnp.einsum("gij,jd->igd", dscore, keys_part, preferred_element_type=jnp.float32)
    key_term = jnp.einsum("gij,igd->jd", dscore, queries, preferred_element_type=jnp.float32)
    value_term = jnp.einsum(
        "gij,igd->jd",
        probabilities.astype(jnp.bfloat16),
        out_grads,
        preferred_element_type=jnp.float32,
    )
    return (query_term, key_term, value_term)


def block_terms(context, keys_part, values_part, key_start):
    queries, out_grads, row_delta, log_sums, block_mask, query_start = context
    tok_rows = queries.shape[0]
    key_count = keys_part.shape[0]
    live_mask = live_region(block_mask, query_start, tok_rows, key_start, key_count)
    return contract(queries, out_grads, row_delta, log_sums, keys_part, values_part, live_mask)


def pass_grads(key_running_total, value_running_total):
    return from_behind((key_running_total, value_running_total), "ctx", -1)


def local(query_rows, key_matrix, value_matrix, attn_out, out_grad, log_sums, block_mask):
    tok_rows = query_rows.shape[0]
    col_width = query_rows.shape[1]
    heads_local = col_width // HEAD_SIZE
    ctx_pos = lax.axis_index("ctx")
    ctx_count = lax.axis_size("ctx")
    tp_pos = lax.axis_index("tp")
    gathered = lax.all_gather(out_grad, "tp", axis=0, tiled=True)
    own_grad = lax.dynamic_slice_in_dim(gathered, tp_pos * col_width, col_width, 1)
    queries = query_rows.reshape(tok_rows, heads_local, HEAD_SIZE)
    out_grads = own_grad.reshape(tok_rows, heads_local, HEAD_SIZE)
    outputs = attn_out.reshape(tok_rows, heads_local, HEAD_SIZE)
    row_delta = jnp.sum(out_grads.astype(jnp.float32) * outputs.astype(jnp.float32), axis=2).T
    query_start = ctx_pos * tok_rows
    context = (queries, out_grads, row_delta, log_sums, block_mask, query_start)
    zero_query = jnp.zeros((tok_rows, heads_local, HEAD_SIZE), jnp.float32)
    zero_key = jnp.zeros((tok_rows, HEAD_SIZE), jnp.float32)

    def visit_turn(turn_index, carried):
        keys_part, values_part, query_acc, key_running_total, value_running_total = carried
        owner_index = jnp.mod(ctx_pos + turn_index, ctx_count)
        query_term, key_term, value_term = block_terms(
            context, keys_part, values_part, owner_index * tok_rows
        )
        key_running_total, value_running_total = pass_grads(
            key_running_total + key_term, value_running_total + value_term
        )
        keys_part, values_part = from_behind((keys_part, values_part), "ctx", -1)
        return (
            keys_part,
            values_part,
            query_acc + query_term,
            key_running_total,
            value_running_total,
        )

    carried = lax.fori_loop(
        0, ctx_count - 1, visit_turn, (key_matrix, value_matrix, zero_query, zero_key, zero_key)
    )
    keys_part, values_part, query_acc, key_running_total, value_running_total = carried
    owner_index = jnp.mod(ctx_pos - 1, ctx_count)
    query_term, key_term, value_term = block_terms(
        context, keys_part, values_part, owner_index * tok_rows
    )
    query_acc = query_acc + query_term
    key_running_total, value_running_total = pass_grads(
        key_running_total + key_term, value_running_total + value_term
    )
    logit_scale = 1.0 / math.sqrt(HEAD_SIZE)
    query_grad = (query_acc * logit_scale).reshape(tok_rows, col_width).astype(jnp.bfloat16)
    key_gradient = (key_running_total * logit_scale).astype(jnp.bfloat16)
    value_gradient = value_running_total.astype(jnp.bfloat16)
    return (query_grad, key_gradient, value_gradient)


def solution(mesh):
    placed = (
        P(("dp", "ctx"), "tp"),
        P(("dp", "ctx"), "tp"),
        P(("dp", "ctx"), "tp"),
        P(("dp", "ctx"), "tp"),
        P(("dp", "ctx", "tp"), None),
        P("tp", ("dp", "ctx")),
        P("dp", None),
    )
    return jax.shard_map(
        local,
        mesh=mesh,
        in_specs=placed,
        out_specs=(P(("dp", "ctx"), "tp"), P(("dp", "ctx"), "tp"), P(("dp", "ctx"), "tp")),
        check_vma=False,
    )
```

profile of v0, /device:TPU:0, one launch (start us, length us, event | category | flops | bytes accessed | tf_op | source)
XLA Modules:
  0.0 88.2 jit_solution(1481765437307424452)
XLA Ops:
  7.2 0.7 all-gather.2.cloned.1.call-update
  7.9 3.0 %collective-permute-start.1 = (bf16[256,128]{1,0:T(8,128)(2,1)}, bf16[256,128]{1,0:T(8,128)(2,1)S(1)}, u32[]{:S(2)}, u32[]{:S(2)}) collective-permute-start(bf16[256,128]{1,0:T(8,128)(2,1)} %param.9), channel_id=1, source_target_pairs={{0,4},{4,0},{1,5},{5,1},{2,6},{6,2},{3,7},{7,3},{8,12},{12,8},{9,1... | collective-permute-start | bytes 196616 | tf_op jit(solution)/shard_map/while/body/eval_jaxpr/ppermute | solution.py:15
  11.0 0.8 dynamic-slice_compare_fusion
  12.6 2.8 %fusion.7 = f32[8,256,256]{1,2,0:T(8,128)} fusion(f32[8,256]{1,0:T(8,128)} %param.12, pred[256,256]{0,1:T(8,128)(4,1)S(1)} %get-tuple-element.41, bf16[256,128]{1,0:T(8,128)(2,1)} %param.8, bf16[256,1024]{1,0:T(8,128)(2,1)S(1)} %copy-done), kind=kOutput, calls=%fused_computation.11 | convolution fusion | flops 135790592 | bytes 2760704 | tf_op jit(solution)/shard_map/while/body/eval_jaxpr/igd,jd->gij/dot_general | solution.py:35
  15.4 1.0 %copy.47 = bf16[256,1024]{0,1:T(8,128)(2,1)} copy(bf16[256,1024]{1,0:T(8,128)(2,1)S(1)} %copy-done.2) | data formatting | bytes 1048576 | tf_op args[3]
  16.4 0.6 fusion.3
  17.0 41.3 %all-gather.2.cloned.1.call-done = bf16[256,4096]{1,0:T(8,128)(2,1)} async-done(((bf16[64,4096]{1,0:T(8,128)(2,1)}), bf16[256,4096]{1,0:T(8,128)(2,1)}) %all-gather.2.cloned.1.call-update) | async-done | bytes 2097168 | tf_op jit(solution)/shard_map/all_gather | solution.py:73
  58.3 1.9 %constant_dynamic-slice_fusion = bf16[256,1024]{1,0:T(8,128)(2,1)} fusion(bf16[256,4096]{1,0:T(8,128)(2,1)} %all-gather.2.cloned.1.call-done, s32[]{:T(128)S(6)} %select_n.83), kind=kLoop, calls=%fused_computation.66 | loop fusion | bytes 1048580 | tf_op jit(solution)/shard_map/dynamic_slice | solution.py:74
  60.2 1.2 %copy.73 = bf16[256,1024]{0,1:T(8,128)(2,1)S(1)} copy(bf16[256,1024]{1,0:T(8,128)(2,1)} %constant_dynamic-slice_fusion) | data formatting | bytes 1048576
  61.5 1.3 %fusion.12 = f32[256,8]{0,1:T(8,128)S(1)} fusion(bf16[256,1024]{0,1:T(8,128)(2,1)} %copy.47, bf16[256,1024]{0,1:T(8,128)(2,1)S(1)} %copy.73), kind=kLoop, calls=%fused_computation.22 | loop fusion | flops 1046528 | bytes 1056768 | tf_op jit(solution)/shard_map/reduce_sum | solution.py:78
  62.8 2.0 %convolution_bitcast_fusion.1 = f32[256,128]{1,0:T(8,128)S(1)} fusion(bf16[256,8,128]{0,2,1:T(8,128)(2,1)S(1)} %bitcast.113, f32[8,256,256]{1,2,0:T(8,128)} %fusion.7), kind=kOutput, calls=%fused_computation.16 | convolution fusion | flops 134742016 | bytes 2752512 | tf_op jit(solution)/shard_map/while/body/eval_jaxpr/gij,igd->jd/dot_general | solution.py:45
  64.9 0.4 fusion.5
  66.0 0.4 convolution_bitcast_fusion.3
  66.5 1.5 %collective-permute-start.2 = (f32[256,128]{1,0:T(8,128)S(1)}, f32[256,128]{1,0:T(8,128)S(1)}, u32[]{:S(2)}, u32[]{:S(2)}) collective-permute-start(f32[256,128]{1,0:T(8,128)S(1)} %convolution_bitcast_fusion.3), channel_id=1, source_target_pairs={{0,4},{4,0},{1,5},{5,1},{2,6},{6,2},{3,7},{7,3},{8,12},{12,8},{9,1... | collective-permute-start | bytes 393224 | tf_op jit(solution)/shard_map/while/body/eval_jaxpr/ppermute | solution.py:15
  68.0 0.6 collective-permute-start.4
  69.0 3.9 %collective-permute-done.2 = f32[256,128]{1,0:T(8,128)S(1)} collective-permute-done((f32[256,128]{1,0:T(8,128)S(1)}, f32[256,128]{1,0:T(8,128)S(1)}, u32[]{:S(2)}, u32[]{:S(2)}) %collective-permute-start.2) | collective-permute-done | bytes 131104 | tf_op jit(solution)/shard_map/while/body/eval_jaxpr/ppermute | solution.py:15
  72.9 0.4 fusion.10
  73.3 1.5 %collective-permute-start.3 = (f32[256,128]{1,0:T(8,128)S(1)}, f32[256,128]{1,0:T(8,128)S(1)}, u32[]{:S(2)}, u32[]{:S(2)}) collective-permute-start(f32[256,128]{1,0:T(8,128)S(1)} %fusion.10), channel_id=1, source_target_pairs={{0,4},{4,0},{1,5},{5,1},{2,6},{6,2},{3,7},{7,3},{8,12},{12,8},{9,1... | collective-permute-start | bytes 393224 | tf_op jit(solution)/shard_map/ppermute | solution.py:15
  75.3 0.4 fusion.11
  75.7 1.5 %collective-permute-start.5 = (bf16[256,128]{1,0:T(8,128)(2,1)S(1)}, bf16[256,128]{1,0:T(8,128)(2,1)S(1)}, u32[]{:S(2)}, u32[]{:S(2)}) collective-permute-start(bf16[256,128]{1,0:T(8,128)(2,1)S(1)} %fusion.11), channel_id=1, source_target_pairs={{0,4},{4,0},{1,5},{5,1},{2,6},{6,2},{3,7},{7,3},{8,12},{12,8},{9,1... | collective-permute-start | bytes 196616 | tf_op jit(solution)/shard_map/ppermute | solution.py:15
  77.6 1.0 %copy.60 = bf16[256,1024]{1,0:T(8,128)(2,1)} copy(bf16[256,1024]{0,1:T(8,128)(2,1)S(1)} %bitcast.117) | data formatting | bytes 1048576
  78.6 1.4 %collective-permute-done.5 = bf16[256,128]{1,0:T(8,128)(2,1)S(1)} collective-permute-done((bf16[256,128]{1,0:T(8,128)(2,1)S(1)}, bf16[256,128]{1,0:T(8,128)(2,1)S(1)}, u32[]{:S(2)}, u32[]{:S(2)}) %collective-permute-start.5) | collective-permute-done | bytes 65568 | tf_op jit(solution)/shard_map/ppermute | solution.py:15
  80.0 0.6 multiply_convert_fusion
  80.7 0.6 copy.96
  (30 shorter events, 2.7 us)
Async XLA Ops:
  7.2 5.4 %copy-start = (bf16[256,1024]{1,0:T(8,128)(2,1)S(1)}, bf16[256,1024]{1,0:T(8,128)(2,1)}, u32[]{:S(2)}) copy-start(bf16[256,1024]{1,0:T(8,128)(2,1)} %param.7) | copy-start | bytes 1572868
  7.2 8.2 %copy-start.2 = (bf16[256,1024]{1,0:T(8,128)(2,1)S(1)}, bf16[256,1024]{1,0:T(8,128)(2,1)}, u32[]{:S(2)}) copy-start(bf16[256,1024]{1,0:T(8,128)(2,1)} %param.10) | copy-start | bytes 1572868
  7.2 51.1 %all-gather.2.cloned.1.call-start = ((), (), s32[]{:S(2)}) async-start(), calls=%async_computation | async-start | bytes 2621440 | tf_op jit(solution)/shard_map/all_gather | solution.py:73
  7.9 60.6 %collective-permute-start.1 = (bf16[256,128]{1,0:T(8,128)(2,1)}, bf16[256,128]{1,0:T(8,128)(2,1)S(1)}, u32[]{:S(2)}, u32[]{:S(2)}) collective-permute-start(bf16[256,128]{1,0:T(8,128)(2,1)} %param.9), channel_id=1, source_target_pairs={{0,4},{4,0},{1,5},{5,1},{2,6},{6,2},{3,7},{7,3},{8,12},{12,8},{9,1... | collective-permute-start | bytes 196616 | tf_op jit(solution)/shard_map/while/body/eval_jaxpr/ppermute | solution.py:15
  11.0 5.4 %collective-permute-start = (bf16[256,128]{1,0:T(8,128)(2,1)}, bf16[256,128]{1,0:T(8,128)(2,1)S(1)}, u32[]{:S(2)}, u32[]{:S(2)}) collective-permute-start(bf16[256,128]{1,0:T(8,128)(2,1)} %param.8), channel_id=1, source_target_pairs={{0,4},{4,0},{1,5},{5,1},{2,6},{6,2},{3,7},{7,3},{8,12},{12,8},{9,1... | collective-permute-start | bytes 196616 | tf_op jit(solution)/shard_map/while/body/eval_jaxpr/ppermute | solution.py:15
  12.5 3.8 %copy-start.5 = (f32[8,256]{1,0:T(8,128)S(1)}, f32[8,256]{1,0:T(8,128)}, u32[]{:S(2)}) copy-start(f32[8,256]{1,0:T(8,128)} %param.12) | copy-start | bytes 24580
  61.4 3.4 %copy-start.1 = (f32[8,256,256]{1,2,0:T(8,128)S(1)}, f32[8,256,256]{1,2,0:T(8,128)}, u32[]{:S(2)}) copy-start(f32[8,256,256]{1,2,0:T(8,128)} %fusion.7) | copy-start | bytes 6291460
  61.4 3.4 %copy-start.3 = (bf16[256,128]{1,0:T(8,128)(2,1)S(1)}, bf16[256,128]{1,0:T(8,128)(2,1)}, u32[]{:S(2)}) copy-start(bf16[256,128]{1,0:T(8,128)(2,1)} %param.9) | copy-start | bytes 196612
  64.8 0.8 copy-start.4
  66.5 6.5 %collective-permute-start.2 = (f32[256,128]{1,0:T(8,128)S(1)}, f32[256,128]{1,0:T(8,128)S(1)}, u32[]{:S(2)}, u32[]{:S(2)}) collective-permute-start(f32[256,128]{1,0:T(8,128)S(1)} %convolution_bitcast_fusion.3), channel_id=1, source_target_pairs={{0,4},{4,0},{1,5},{5,1},{2,6},{6,2},{3,7},{7,3},{8,12},{12,8},{9,1... | collective-permute-start | bytes 393224 | tf_op jit(solution)/shard_map/while/body/eval_jaxpr/ppermute | solution.py:15
  68.0 7.3 %collective-permute-start.4 = (f32[256,128]{1,0:T(8,128)S(1)}, f32[256,128]{1,0:T(8,128)S(1)}, u32[]{:S(2)}, u32[]{:S(2)}) collective-permute-start(f32[256,128]{1,0:T(8,128)S(1)} %convolution_bitcast_fusion.1), channel_id=1, source_target_pairs={{0,4},{4,0},{1,5},{5,1},{2,6},{6,2},{3,7},{7,3},{8,12},{12,8},{9,1... | collective-permute-start | bytes 393224 | tf_op jit(solution)/shard_map/while/body/eval_jaxpr/ppermute | solution.py:15
  73.3 6.7 %collective-permute-start.3 = (f32[256,128]{1,0:T(8,128)S(1)}, f32[256,128]{1,0:T(8,128)S(1)}, u32[]{:S(2)}, u32[]{:S(2)}) collective-permute-start(f32[256,128]{1,0:T(8,128)S(1)} %fusion.10), channel_id=1, source_target_pairs={{0,4},{4,0},{1,5},{5,1},{2,6},{6,2},{3,7},{7,3},{8,12},{12,8},{9,1... | collective-permute-start | bytes 393224 | tf_op jit(solution)/shard_map/ppermute | solution.py:15
  75.7 4.3 %collective-permute-start.5 = (bf16[256,128]{1,0:T(8,128)(2,1)S(1)}, bf16[256,128]{1,0:T(8,128)(2,1)S(1)}, u32[]{:S(2)}, u32[]{:S(2)}) collective-permute-start(bf16[256,128]{1,0:T(8,128)(2,1)S(1)} %fusion.11), channel_id=1, source_target_pairs={{0,4},{4,0},{1,5},{5,1},{2,6},{6,2},{3,7},{7,3},{8,12},{12,8},{9,1... | collective-permute-start | bytes 196616 | tf_op jit(solution)/shard_map/ppermute | solution.py:15
Sparse Core Ops, SparseCore 0:
  9.6 48.6 all-gather.1
where the time goes:
time: 88.5 us; the launch traced here: 88.2 us
  waiting for transfers between devices  47.7 us (54%)
  between operations  14.2 us (16%)
  starting transfers between devices  8.31 us (9%)
  matrix products  8.28 us (9%)
  local copies, waits for them, and re-layouts  6.54 us (7%)
  other arithmetic  3.09 us (3%)
    all_gather x1, waiting for transfers between devices, local(): gathered = lax.all_gather(out_grad, 'tp', axis=0, tiled=True)  41.3 us
    ppermute x6, starting transfers between devices, from_behind(): return lax.ppermute(value, axis, pairs)  8.27 us
    ppermute x6, waiting for transfers between devices, from_behind(): return lax.ppermute(value, axis, pairs)  5.74 us
    unnamed x18, local copies, waits for them, and re-layouts  4.44 us
    dot_general x2, matrix products, contract(): jnp.einsum('igd,jd->gij', queries, keys_part, preferred_element_type=jnp....  3.41 us
    dot_general x2, matrix products, contract(): jnp.einsum('gij,igd->jd', probabilities.astype(jnp.bfloat16), out_grads,...  2.45 us
    dynamic_slice x1, local copies, waits for them, and re-layouts, local(): lax.dynamic_slice_in_dim(gathered, tp_pos * col_width, col_width, 1)  1.87 us
  transfers between devices with their start and end apart: 7, of which 4 were waited for; matrix products, arithmetic and copies ran while one was open for 18% of the time, Pallas kernels for 0%

commit v1 on v0

v1 whole, which is shorter than its diff:
```python
import functools
import math

import jax
import jax.numpy as jnp
from jax import lax
from jax.experimental import pallas as pl
from jax.experimental.pallas import tpu as pltpu
from jax.sharding import PartitionSpec as P

BLK = 128
HEAD_SIZE = 128
MESH = pl.DeviceIdType.MESH
BF16 = jnp.bfloat16
F32 = jnp.float32


def dot(a, b, dims=((1,), (0,))):
    return lax.dot_general(a, b, (dims, ((), ())), preferred_element_type=F32)


def partner(me, k, count):
    if count == 4:
        if k == 1:
            return me + 1 - 2 * lax.rem(me, 2)
        if k == 2:
            return lax.rem(me + 2, 4)
        return 3 - me
    return lax.rem(me + k, count)


def source_of(me, k, count):
    if count == 4:
        return partner(me, k, count)
    return lax.rem(me + count - k, count)


def kernel(
    n, tp,
    q_hbm, k_hbm, v_hbm, o_hbm, g_hbm, lse_hbm, mask_ref,
    dq_hbm, dk_hbm, dv_hbm,
    q, o, g, lse, kb, vb, vx, lcol, lhs, p, pt, qt, dq_acc, dq_st, dkt, dva,
    dk_send, dv_send, dk_recv, dv_recv, dk_st, dv_st,
    load_sem, out_sem, g_send, g_recv, kv_send, kv_recv, d_send, d_recv,
):
    c = lax.axis_index("ctx")
    me = lax.axis_index("tp")
    tokens = q.shape[0]
    heads = q.shape[1] // HEAD_SIZE
    rows = tokens // tp
    span_blocks = tokens // BLK
    chunk_per_block = BLK // rows
    width = heads * HEAD_SIZE
    scale = 1.0 / math.sqrt(HEAD_SIZE)

    def chunk_rows(s):
        return pl.ds(pl.multiple_of(s * rows, rows), rows)

    loads = [
        pltpu.make_async_copy(src, dst, load_sem.at[i])
        for i, (src, dst) in enumerate(
            [
                (q_hbm, q),
                (k_hbm, kb.at[0]),
                (lse_hbm, lse),
                (v_hbm, vb.at[0]),
                (o_hbm, o),
                (
                    g_hbm.at[:, pl.ds(pl.multiple_of(me * width, width), width)],
                    g.at[chunk_rows(me)],
                ),
            ]
        )
    ]
    for load in loads:
        load.start()

    barrier = pltpu.get_barrier_semaphore()
    for k in range(1, tp):
        pl.semaphore_signal(
            barrier, inc=1, device_id={"tp": lax.rem(me + k, tp)}, device_id_type=MESH
        )
    for d in range(1, n):
        pl.semaphore_signal(
            barrier, inc=1, device_id={"ctx": lax.rem(c + d, n)}, device_id_type=MESH
        )
    pl.semaphore_wait(barrier, tp - 1 + n - 1)

    def grad_copy(k):
        to = partner(me, k, tp)
        return pltpu.make_async_remote_copy(
            src_ref=g_hbm.at[:, pl.ds(pl.multiple_of(to * width, width), width)],
            dst_ref=g.at[chunk_rows(me)],
            send_sem=g_send.at[k - 1],
            recv_sem=g_recv.at[k - 1],
            device_id={"tp": to},
            device_id_type=MESH,
        )

    def grad_arrival(k):
        return pltpu.make_async_remote_copy(
            src_ref=g_hbm.at[:, pl.ds(0, width)],
            dst_ref=g.at[chunk_rows(source_of(me, k, tp))],
            send_sem=g_send.at[k - 1],
            recv_sem=g_recv.at[k - 1],
            device_id={"tp": source_of(me, k, tp)},
            device_id_type=MESH,
        )

    order = (2, 3, 1) if tp == 4 else tuple(range(1, tp))
    for k in order:
        grad_copy(k).start()

    def kv_copies(d):
        to = lax.rem(c + d, n)
        return [
            pltpu.make_async_remote_copy(
                src_ref=src,
                dst_ref=dst.at[d],
                send_sem=kv_send.at[i, d - 1],
                recv_sem=kv_recv.at[i, d - 1],
                device_id={"ctx": to},
                device_id_type=MESH,
            )
            for i, (src, dst) in enumerate([(k_hbm, kb), (v_hbm, vb)])
        ]

    for d in range(1, n):

        @pl.when(c + d < n)
        def _():
            for copy in kv_copies(d):
                copy.start()

    def stack(ref, s):
        return jnp.concatenate(
            [
                ref[chunk_rows(s), h * HEAD_SIZE : (h + 1) * HEAD_SIZE]
                for h in range(heads)
            ],
            axis=0,
        )

    def span_probs(slot, d, own):
        keys = kb[d]
        vx[slot, :, 0:HEAD_SIZE] = vb[d]
        key_at = lax.broadcasted_iota(jnp.int32, (rows, tokens), 1)
        row_at = lax.broadcasted_iota(jnp.int32, (rows, tokens), 0)
        key_block = key_at // BLK
        for s in range(tp):
            block = s // chunk_per_block
            table = jnp.zeros((rows, tokens), jnp.int32)
            for b in range(span_blocks if not own else block):
                allowed = mask_ref[c * span_blocks + block, (c - d) * span_blocks + b]
                table = jnp.where(key_block == b, allowed, table)
            live = table == 1
            if own:
                live = live | ((key_block == block) & (key_at <= row_at + s * rows))
            scores = dot(stack(q, s), keys, ((1,), (1,)))
            for h in range(heads):
                part = scores[h * rows : (h + 1) * rows] * scale
                col = lcol[s * rows : (s + 1) * rows, h : h + 1]
                p[slot, s, h * rows : (h + 1) * rows, :] = jnp.where(
                    live, jnp.exp(part - col), 0.0
                )
            pt[slot, s] = p[slot, s].T.astype(BF16)

    def chunk_lhs(s):
        grads = stack(g, s)
        product = grads.astype(F32) * stack(o, s).astype(F32)
        high = product.astype(BF16)
        low = (product - high.astype(F32)).astype(BF16)
        lhs[s] = jnp.concatenate([grads, high, low], axis=1)

    def chunk_terms(slot, d, s):
        inner = dot(lhs[s], vx[slot], ((1,), (1,)))
        dscore = (p[slot, s] * inner).astype(BF16)
        dkt[slot] += dot(qt[s], dscore)
        dva[slot] += dot(pt[slot, s], lhs[s, :, 0:HEAD_SIZE])
        return dot(dscore, kb[d])

    def out_copy(s, i):
        return pltpu.make_async_copy(
            dq_st.at[chunk_rows(s)], dq_hbm.at[chunk_rows(s)], out_sem.at[i]
        )

    def finish_query(s, total, i):
        grad = (total * scale).astype(BF16)
        for h in range(heads):
            dq_st[chunk_rows(s), h * HEAD_SIZE : (h + 1) * HEAD_SIZE] = grad[
                h * rows : (h + 1) * rows
            ]
        out_copy(s, i).start()

    def partial_copies(d):
        to = lax.rem(c - d + n, n)
        return [
            pltpu.make_async_remote_copy(
                src_ref=src.at[d - 1],
                dst_ref=dst.at[d - 1],
                send_sem=d_send.at[i, d - 1],
                recv_sem=d_recv.at[i, d - 1],
                device_id={"ctx": to},
                device_id_type=MESH,
            )
            for i, (src, dst) in enumerate([(dk_send, dk_recv), (dv_send, dv_recv)])
        ]

    def send_partials(d):
        dk_send[d - 1] = dkt[1].astype(BF16)
        dv_send[d - 1] = dva[1].astype(BF16)
        for copy in partial_copies(d):
            copy.start()

    dkt[...] = jnp.zeros_like(dkt)
    dva[...] = jnp.zeros_like(dva)
    dq_acc[...] = jnp.zeros_like(dq_acc)
    vx[:, :, HEAD_SIZE:] = jnp.full((2, tokens, 2 * HEAD_SIZE), -1.0, BF16)
    for load in loads:
        load.wait()
    lcol[...] = lse[...].T
    for s in range(tp):
        qt[s] = stack(q, s).T
    span_probs(0, 0, True)

    @pl.when(c >= 1)
    def _():
        for copy in kv_copies(1):
            copy.wait_recv()
        span_probs(1, 1, False)

    steps = (0,) + ((1, 2, 3) if tp == 4 else tuple(range(1, tp)))
    for i, k in enumerate(steps):
        if k == 0:
            s = me
        else:
            s = source_of(me, k, tp)
            grad_arrival(k).wait_recv()
        chunk_lhs(s)

        @pl.when(c >= 1)
        def _():
            dq_acc[s] += chunk_terms(1, 1, s)
            if i == tp - 1:
                send_partials(1)

        total = dq_acc[s] + chunk_terms(0, 0, s)
        if n == 2:
            finish_query(s, total, i)
        else:
            dq_acc[s] = total

    if n > 2:

        @pl.loop(2, n)
        def _(d):
            @pl.when(c >= d)
            def _():
                for copy in kv_copies(d):
                    copy.wait_recv()
                dkt[1] = jnp.zeros(dkt.shape[1:], F32)
                dva[1] = jnp.zeros(dva.shape[1:], F32)
                span_probs(1, d, False)
                for s in range(tp):
                    dq_acc[s] += chunk_terms(1, d, s)
                send_partials(d)

        for s in range(tp):
            finish_query(s, dq_acc[s], s)

    for d in range(1, n):

        @pl.when(c + d < n)
        def _():
            for copy in partial_copies(d):
                copy.wait_recv()
            dkt[0] += dk_recv[d - 1].astype(F32)
            dva[0] += dv_recv[d - 1].astype(F32)

    dk_st[...] = (dkt[0] * scale).T.astype(BF16)
    dv_st[...] = dva[0].astype(BF16)
    ends = [
        pltpu.make_async_copy(dk_st, dk_hbm, out_sem.at[tp]),
        pltpu.make_async_copy(dv_st, dv_hbm, out_sem.at[tp + 1]),
    ]
    for copy in ends:
        copy.start()

    for k in range(1, tp):
        grad_copy(k).wait_send()
    for d in range(1, n):

        @pl.when(c + d < n)
        def _():
            for copy in kv_copies(d):
                copy.wait_send()

        @pl.when(c >= d)
        def _():
            for copy in partial_copies(d):
                copy.wait_send()

    for i, k in enumerate(steps):
        if n == 2:
            out_copy(me if k == 0 else source_of(me, k, tp), i).wait()
        else:
            out_copy(i, i).wait()
    for copy in ends:
        copy.wait()


def local(query_rows, key_matrix, value_matrix, attn_out, out_grad, log_sums, block_mask):
    tokens, width = query_rows.shape
    heads = width // HEAD_SIZE
    n = lax.axis_size("ctx")
    tp = lax.axis_size("tp")
    rows = tokens // tp
    stacked = heads * rows
    vmem = pltpu.VMEM
    dma = pltpu.SemaphoreType.DMA
    anywhere = pl.BlockSpec(memory_space=pl.ANY)
    return pl.pallas_call(
        functools.partial(kernel, n, tp),
        out_shape=(
            jax.ShapeDtypeStruct((tokens, width), BF16),
            jax.ShapeDtypeStruct((tokens, HEAD_SIZE), BF16),
            jax.ShapeDtypeStruct((tokens, HEAD_SIZE), BF16),
        ),
        in_specs=[anywhere] * 6 + [pl.BlockSpec(memory_space=pltpu.SMEM)],
        out_specs=(anywhere,) * 3,
        scratch_shapes=[
            vmem((tokens, width), BF16),
            vmem((tokens, width), BF16),
            vmem((tokens, width), BF16),
            vmem((heads, tokens), F32),
            vmem((n, tokens, HEAD_SIZE), BF16),
            vmem((n, tokens, HEAD_SIZE), BF16),
            vmem((2, tokens, 3 * HEAD_SIZE), BF16),
            vmem((tokens, heads), F32),
            vmem((tp, stacked, 3 * HEAD_SIZE), BF16),
            vmem((2, tp, stacked, tokens), F32),
            vmem((2, tp, tokens, stacked), BF16),
            vmem((tp, HEAD_SIZE, stacked), BF16),
            vmem((tp, stacked, HEAD_SIZE), F32),
            vmem((tokens, width), BF16),
            vmem((2, HEAD_SIZE, tokens), F32),
            vmem((2, tokens, HEAD_SIZE), F32),
            vmem((n - 1, HEAD_SIZE, tokens), BF16),
            vmem((n - 1, tokens, HEAD_SIZE), BF16),
            vmem((n - 1, HEAD_SIZE, tokens), BF16),
            vmem((n - 1, tokens, HEAD_SIZE), BF16),
            vmem((tokens, HEAD_SIZE), BF16),
            vmem((tokens, HEAD_SIZE), BF16),
            dma((6,)),
            dma((tp + 2,)),
            dma((tp - 1,)),
            dma((tp - 1,)),
            dma((2, n - 1)),
            dma((2, n - 1)),
            dma((2, n - 1)),
            dma((2, n - 1)),
        ],
        compiler_params=pltpu.CompilerParams(
            collective_id=0, has_side_effects=True, vmem_limit_bytes=48 * 1024 * 1024
        ),
    )(query_rows, key_matrix, value_matrix, attn_out, out_grad, log_sums, block_mask)


def solution(mesh):
    placed = (
        P(("dp", "ctx"), "tp"),
        P(("dp", "ctx"), "tp"),
        P(("dp", "ctx"), "tp"),
        P(("dp", "ctx"), "tp"),
        P(("dp", "ctx", "tp"), None),
        P("tp", ("dp", "ctx")),
        P("dp", None),
    )
    return jax.shard_map(
        local,
        mesh=mesh,
        in_specs=placed,
        out_specs=(P(("dp", "ctx"), "tp"), P(("dp", "ctx"), "tp"), P(("dp", "ctx"), "tp")),
        check_vma=False,
    )
```

time: 88.5 us -> 33.3 us (0.38)
  waiting for transfers between devices: 47.7 us -> 0 us
  Pallas kernels: 0 us -> 24 us
  between operations: 14.2 us -> 0.66 us
  starting transfers between devices: 8.31 us -> 0 us
  matrix products: 8.28 us -> 0 us
  other arithmetic: 3.09 us -> 0 us
  local copies, waits for them, and re-layouts: 6.54 us -> 8.23 us
    all_gather x1 -> x0, waiting for transfers between devices: 41.3 us -> none  [local(): gathered = lax.all_gather(out_grad, 'tp', axis=0, tiled=True)]
    pallas_call x0 -> x1, Pallas kernels: none -> 24 us  [local(): pl.pallas_call(functools.partial(kernel, n, tp), out_shape=(jax.ShapeDtyp...]
    dot_general x10 -> x0, matrix products: 8.28 us -> none  [the longest x2 3.41 us: contract(): jnp.einsum('igd,jd->gij', queries, keys_part, preferred_element_type=jnp....]
    ppermute x6 -> x0, starting transfers between devices: 8.27 us -> none  [from_behind(): return lax.ppermute(value, axis, pairs)]
    ppermute x6 -> x0, waiting for transfers between devices: 5.74 us -> none  [from_behind(): return lax.ppermute(value, axis, pairs)]
    unnamed x18 -> x17, local copies, waits for them, and re-layouts: 4.44 us -> 8.23 us
    dynamic_slice x1 -> x0, local copies, waits for them, and re-layouts: 1.87 us -> none  [local(): lax.dynamic_slice_in_dim(gathered, tp_pos * col_width, col_width, 1)]
    reduce_sum x1 -> x0, other arithmetic: 1.34 us -> none  [local(): jnp.sum(out_grads.astype(jnp.float32) * outputs.astype(jnp.float32), axis=2)]
  transfers between devices with their start and end apart: 7 -> 0, of which waited for: 4 -> 0; matrix products, arithmetic and copies ran while one was open for 18% -> 0% of each run, Pallas kernels for 0% -> 0%
where the time goes in v1:
time: 33.3 us; the launch traced here: 32.9 us
  Pallas kernels  24 us (72%)
  local copies, waits for them, and re-layouts  8.23 us (25%)
  between operations  0.66 us (2%)
    pallas_call x1, Pallas kernels, local(): pl.pallas_call(functools.partial(kernel, n, tp), out_shape=(jax.ShapeDtyp...  24 us
    unnamed x17, local copies, waits for them, and re-layouts  8.23 us

profile of v1, /device:TPU:0, one launch (start us, length us, event | category | flops | bytes accessed | tf_op | source)
XLA Modules:
  0.0 32.9 jit_solution(5984921105180640143)
XLA Ops:
  0.6 0.0 copy-start
  0.6 1.0 %copy-done = bf16[256,1024]{1,0:T(8,128)(2,1)S(1)} copy-done((bf16[256,1024]{1,0:T(8,128)(2,1)S(1)}, bf16[256,1024]{1,0:T(8,128)(2,1)}, u32[]{:S(2)}) %copy-start) | copy-done | bytes 524312
  1.7 0.0 copy-start.1
  1.7 1.0 %copy-done.1 = bf16[256,1024]{1,0:T(8,128)(2,1)S(1)} copy-done((bf16[256,1024]{1,0:T(8,128)(2,1)S(1)}, bf16[256,1024]{1,0:T(8,128)(2,1)}, u32[]{:S(2)}) %copy-start.1) | copy-done | bytes 524312
  2.7 0.0 copy-start.2
  2.7 1.0 %copy-done.2 = bf16[64,4096]{1,0:T(8,128)(2,1)S(1)} copy-done((bf16[64,4096]{1,0:T(8,128)(2,1)S(1)}, bf16[64,4096]{1,0:T(8,128)(2,1)}, u32[]{:S(2)}) %copy-start.2) | copy-done | bytes 524312
  3.8 0.0 copy-start.3
  3.8 0.8 %copy-done.3 = bf16[256,128]{1,0:T(8,128)(2,1)S(1)} copy-done((bf16[256,128]{1,0:T(8,128)(2,1)S(1)}, bf16[256,128]{1,0:T(8,128)(2,1)}, u32[]{:S(2)}) %copy-start.3) | copy-done | bytes 65560
  4.6 0.0 copy-start.4
  4.6 0.8 %copy-done.4 = bf16[256,128]{1,0:T(8,128)(2,1)S(1)} copy-done((bf16[256,128]{1,0:T(8,128)(2,1)S(1)}, bf16[256,128]{1,0:T(8,128)(2,1)}, u32[]{:S(2)}) %copy-start.4) | copy-done | bytes 65560
  5.4 0.0 copy-start.5
  5.4 0.7 %copy-done.5 = f32[8,256]{1,0:T(8,128)S(1)} copy-done((f32[8,256]{1,0:T(8,128)S(1)}, f32[8,256]{1,0:T(8,128)}, u32[]{:S(2)}) %copy-start.5) | copy-done | bytes 8216
  6.1 0.0 copy-start.6
  6.1 0.7 %copy-done.6 = s32[4,4]{1,0:T(4,128)S(1)} copy-done((s32[4,4]{1,0:T(4,128)S(1)}, s32[4,4]{1,0:T(4,128)}, u32[]{:S(2)}) %copy-start.6) | copy-done | bytes 88
  6.8 24.0 %shard_map.94 = (bf16[256,1024]{1,0:T(8,128)(2,1)S(1)}, bf16[256,128]{1,0:T(8,128)(2,1)S(1)}, bf16[256,128]{1,0:T(8,128)(2,1)S(1)}) custom-call(bf16[256,1024]{1,0:T(8,128)(2,1)S(1)} %copy-done, bf16[256,128]{1,0:T(8,128)(2,1)S(1)} %copy-done.3, bf16[256,128]{1,0:T(8,128)(2,1)S(1)} %copy-done.4, bf16[256,1024]{1,0:T(8,128)(2,1)S(1)} %copy-done.1, ...), custom_call_target="tpu_custom_call" | custom-call | tf_op jit(solution)/shard_map/pallas_call | solution.py:322
  30.8 0.8 %copy.13 = bf16[256,1024]{1,0:T(8,128)(2,1)} copy(bf16[256,1024]{1,0:T(8,128)(2,1)S(1)} %get-tuple-element.6) | data formatting | bytes 1048576
  31.6 0.6 %copy.14 = bf16[256,128]{1,0:T(8,128)(2,1)} copy(bf16[256,128]{1,0:T(8,128)(2,1)S(1)} %get-tuple-element.7) | data formatting | bytes 131072
  32.2 0.6 %copy.15 = bf16[256,128]{1,0:T(8,128)(2,1)} copy(bf16[256,128]{1,0:T(8,128)(2,1)S(1)} %get-tuple-element.8) | data formatting | bytes 131072
Async XLA Ops:
  0.6 1.0 %copy-start = (bf16[256,1024]{1,0:T(8,128)(2,1)S(1)}, bf16[256,1024]{1,0:T(8,128)(2,1)}, u32[]{:S(2)}) copy-start(bf16[256,1024]{1,0:T(8,128)(2,1)} %q_hbm.1) | copy-start | bytes 1572868
  1.7 1.0 %copy-start.1 = (bf16[256,1024]{1,0:T(8,128)(2,1)S(1)}, bf16[256,1024]{1,0:T(8,128)(2,1)}, u32[]{:S(2)}) copy-start(bf16[256,1024]{1,0:T(8,128)(2,1)} %o_hbm.1) | copy-start | bytes 1572868
  2.7 1.0 %copy-start.2 = (bf16[64,4096]{1,0:T(8,128)(2,1)S(1)}, bf16[64,4096]{1,0:T(8,128)(2,1)}, u32[]{:S(2)}) copy-start(bf16[64,4096]{1,0:T(8,128)(2,1)} %g_hbm.1) | copy-start | bytes 1572868
  3.8 0.8 %copy-start.3 = (bf16[256,128]{1,0:T(8,128)(2,1)S(1)}, bf16[256,128]{1,0:T(8,128)(2,1)}, u32[]{:S(2)}) copy-start(bf16[256,128]{1,0:T(8,128)(2,1)} %k_hbm.1) | copy-start | bytes 196612
  4.6 0.8 %copy-start.4 = (bf16[256,128]{1,0:T(8,128)(2,1)S(1)}, bf16[256,128]{1,0:T(8,128)(2,1)}, u32[]{:S(2)}) copy-start(bf16[256,128]{1,0:T(8,128)(2,1)} %v_hbm.1) | copy-start | bytes 196612
  5.4 0.7 %copy-start.5 = (f32[8,256]{1,0:T(8,128)S(1)}, f32[8,256]{1,0:T(8,128)}, u32[]{:S(2)}) copy-start(f32[8,256]{1,0:T(8,128)} %lse_hbm.1) | copy-start | bytes 24580
  6.1 0.7 %copy-start.6 = (s32[4,4]{1,0:T(4,128)S(1)}, s32[4,4]{1,0:T(4,128)}, u32[]{:S(2)}) copy-start(s32[4,4]{1,0:T(4,128)} %mask_ref.1) | copy-start | bytes 196

commit v2 on v1

--- a/solution.py
+++ b/solution.py
@@ -37,11 +37,11 @@
 
 def kernel(
     n, tp,
-    q_hbm, k_hbm, v_hbm, o_hbm, g_hbm, lse_hbm, mask_ref,
-    dq_hbm, dk_hbm, dv_hbm,
-    q, o, g, lse, kb, vb, vx, lcol, lhs, p, pt, qt, dq_acc, dq_st, dkt, dva,
-    dk_send, dv_send, dk_recv, dv_recv, dk_st, dv_st,
-    load_sem, out_sem, g_send, g_recv, kv_send, kv_recv, d_send, d_recv,
+    q_hbm, k_hbm, v_hbm, o_hbm, g_hbm, lse_hbm, mask_hbm,
+    dq_st, dk_st, dv_st,
+    q, o, g, lse, kb, vb, vx, lcol, lhs, p, pt, qt, dq_acc, dkt, dva,
+    dk_send, dv_send, dk_recv, dv_recv, mask_ref,
+    load_sem, g_send, g_recv, kv_send, kv_recv, d_send, d_recv,
 ):
     c = lax.axis_index("ctx")
     me = lax.axis_index("tp")
@@ -60,6 +60,7 @@
         pltpu.make_async_copy(src, dst, load_sem.at[i])
         for i, (src, dst) in enumerate(
             [
+                (mask_hbm, mask_ref),
                 (q_hbm, q),
                 (k_hbm, kb.at[0]),
                 (lse_hbm, lse),
@@ -107,7 +108,7 @@
             device_id_type=MESH,
         )
 
-    order = (2, 3, 1) if tp == 4 else tuple(range(1, tp))
+    order = (1, 2, 3) if tp == 4 else tuple(range(1, tp))
     for k in order:
         grad_copy(k).start()
 
@@ -165,32 +166,31 @@
                 )
             pt[slot, s] = p[slot, s].T.astype(BF16)
 
-    def chunk_lhs(s):
-        grads = stack(g, s)
+    def chunk_lhs(s, grads):
         product = grads.astype(F32) * stack(o, s).astype(F32)
         high = product.astype(BF16)
         low = (product - high.astype(F32)).astype(BF16)
         lhs[s] = jnp.concatenate([grads, high, low], axis=1)
 
-    def chunk_terms(slot, d, s):
+    def value_term(slot, s, grads):
+        dva[slot] += dot(pt[slot, s], grads)
+
+    def key_term(slot, s):
         inner = dot(lhs[s], vx[slot], ((1,), (1,)))
         dscore = (p[slot, s] * inner).astype(BF16)
         dkt[slot] += dot(qt[s], dscore)
-        dva[slot] += dot(pt[slot, s], lhs[s, :, 0:HEAD_SIZE])
-        return dot(dscore, kb[d])
-
-    def out_copy(s, i):
-        return pltpu.make_async_copy(
-            dq_st.at[chunk_rows(s)], dq_hbm.at[chunk_rows(s)], out_sem.at[i]
-        )
-
-    def finish_query(s, total, i):
+        return dscore
+
+    def chunk_terms(slot, d, s):
+        value_term(slot, s, lhs[s, :, 0:HEAD_SIZE])
+        return dot(key_term(slot, s), kb[d])
+
+    def finish_query(s, total):
         grad = (total * scale).astype(BF16)
         for h in range(heads):
             dq_st[chunk_rows(s), h * HEAD_SIZE : (h + 1) * HEAD_SIZE] = grad[
                 h * rows : (h + 1) * rows
             ]
-        out_copy(s, i).start()
 
     def partial_copies(d):
         to = lax.rem(c - d + n, n)
@@ -206,11 +206,13 @@
             for i, (src, dst) in enumerate([(dk_send, dk_recv), (dv_send, dv_recv)])
         ]
 
-    def send_partials(d):
+    def send_value_partial(d):
+        dv_send[d - 1] = dva[1].astype(BF16)
+        partial_copies(d)[1].start()
+
+    def send_key_partial(d):
         dk_send[d - 1] = dkt[1].astype(BF16)
-        dv_send[d - 1] = dva[1].astype(BF16)
-        for copy in partial_copies(d):
-            copy.start()
+        partial_copies(d)[0].start()
 
     dkt[...] = jnp.zeros_like(dkt)
     dva[...] = jnp.zeros_like(dva)
@@ -236,17 +238,31 @@
         else:
             s = source_of(me, k, tp)
             grad_arrival(k).wait_recv()
-        chunk_lhs(s)
-
-        @pl.when(c >= 1)
-        def _():
-            dq_acc[s] += chunk_terms(1, 1, s)
-            if i == tp - 1:
-                send_partials(1)
+        grads = stack(g, s)
+        if i < tp - 1:
+            chunk_lhs(s, grads)
+
+            @pl.when(c >= 1)
+            def _():
+                dq_acc[s] += chunk_terms(1, 1, s)
+
+        else:
+            @pl.when(c >= 1)
+            def _():
+                value_term(1, s, grads)
+                send_value_partial(1)
+
+            chunk_lhs(s, grads)
+
+            @pl.when(c >= 1)
+            def _():
+                dscore = key_term(1, s)
+                send_key_partial(1)
+                dq_acc[s] += dot(dscore, kb[1])
 
         total = dq_acc[s] + chunk_terms(0, 0, s)
         if n == 2:
-            finish_query(s, total, i)
+            finish_query(s, total)
         else:
             dq_acc[s] = total
 
@@ -263,29 +279,24 @@
                 span_probs(1, d, False)
                 for s in range(tp):
                     dq_acc[s] += chunk_terms(1, d, s)
-                send_partials(d)
+                send_value_partial(d)
+                send_key_partial(d)
 
         for s in range(tp):
-            finish_query(s, dq_acc[s], s)
+            finish_query(s, dq_acc[s])
 
     for d in range(1, n):
 
         @pl.when(c + d < n)
         def _():
-            for copy in partial_copies(d):
-                copy.wait_recv()
+            keys_in, values_in = partial_copies(d)
+            values_in.wait_recv()
+            dva[0] += dv_recv[d - 1].astype(F32)
+            keys_in.wait_recv()
             dkt[0] += dk_recv[d - 1].astype(F32)
-            dva[0] += dv_recv[d - 1].astype(F32)
 
     dk_st[...] = (dkt[0] * scale).T.astype(BF16)
     dv_st[...] = dva[0].astype(BF16)
-    ends = [
-        pltpu.make_async_copy(dk_st, dk_hbm, out_sem.at[tp]),
-        pltpu.make_async_copy(dv_st, dv_hbm, out_sem.at[tp + 1]),
-    ]
-    for copy in ends:
-        copy.start()
-
     for k in range(1, tp):
         grad_copy(k).wait_send()
     for d in range(1, n):
@@ -299,14 +310,6 @@
         def _():
             for copy in partial_copies(d):
                 copy.wait_send()
-
-    for i, k in enumerate(steps):
-        if n == 2:
-            out_copy(me if k == 0 else source_of(me, k, tp), i).wait()
-        else:
-            out_copy(i, i).wait()
-    for copy in ends:
-        copy.wait()
 
 
 def local(query_rows, key_matrix, value_matrix, attn_out, out_grad, log_sums, block_mask):
@@ -318,16 +321,16 @@
     stacked = heads * rows
     vmem = pltpu.VMEM
     dma = pltpu.SemaphoreType.DMA
-    anywhere = pl.BlockSpec(memory_space=pl.ANY)
+    hbm = pl.BlockSpec(memory_space=pltpu.HBM)
     return pl.pallas_call(
         functools.partial(kernel, n, tp),
         out_shape=(
-            jax.ShapeDtypeStruct((tokens, width), BF16),
-            jax.ShapeDtypeStruct((tokens, HEAD_SIZE), BF16),
-            jax.ShapeDtypeStruct((tokens, HEAD_SIZE), BF16),
+            vmem((tokens, width), BF16),
+            vmem((tokens, HEAD_SIZE), BF16),
+            vmem((tokens, HEAD_SIZE), BF16),
         ),
-        in_specs=[anywhere] * 6 + [pl.BlockSpec(memory_space=pltpu.SMEM)],
-        out_specs=(anywhere,) * 3,
+        in_specs=[hbm] * 7,
+        out_specs=(pl.BlockSpec(memory_space=pltpu.VMEM),) * 3,
         scratch_shapes=[
             vmem((tokens, width), BF16),
             vmem((tokens, width), BF16),
@@ -342,17 +345,14 @@
             vmem((2, tp, tokens, stacked), BF16),
             vmem((tp, HEAD_SIZE, stacked), BF16),
             vmem((tp, stacked, HEAD_SIZE), F32),
-            vmem((tokens, width), BF16),
             vmem((2, HEAD_SIZE, tokens), F32),
             vmem((2, tokens, HEAD_SIZE), F32),
             vmem((n - 1, HEAD_SIZE, tokens), BF16),
             vmem((n - 1, tokens, HEAD_SIZE), BF16),
             vmem((n - 1, HEAD_SIZE, tokens), BF16),
             vmem((n - 1, tokens, HEAD_SIZE), BF16),
-            vmem((tokens, HEAD_SIZE), BF16),
-            vmem((tokens, HEAD_SIZE), BF16),
-            dma((6,)),
-            dma((tp + 2,)),
+            pltpu.SMEM(block_mask.shape, jnp.int32),
+            dma((7,)),
             dma((tp - 1,)),
             dma((tp - 1,)),
             dma((2, n - 1)),
@@ -361,7 +361,7 @@
             dma((2, n - 1)),
         ],
         compiler_params=pltpu.CompilerParams(
-            collective_id=0, has_side_effects=True, vmem_limit_bytes=48 * 1024 * 1024
+            collective_id=0, has_side_effects=True, vmem_limit_bytes=62 * 1024 * 1024
         ),
     )(query_rows, key_matrix, value_matrix, attn_out, out_grad, log_sums, block_mask)
 

time: 33.3 us -> 25.3 us (0.76)
  local copies, waits for them, and re-layouts: 8.23 us -> 2.05 us
  Pallas kernels: 24 us -> 22.5 us
    unnamed x17 -> x3, local copies, waits for them, and re-layouts: 8.23 us -> 2.05 us
    pallas_call x1, Pallas kernels: 24 us -> 22.5 us  [local(): pl.pallas_call(functools.partial(kernel, n, tp), out_shape=(vmem((tokens,...]
where the time goes in v2:
time: 25.3 us; the launch traced here: 25.2 us
  Pallas kernels  22.5 us (89%)
  local copies, waits for them, and re-layouts  2.05 us (8%)
  between operations  0.64 us (3%)
    pallas_call x1, Pallas kernels, local(): pl.pallas_call(functools.partial(kernel, n, tp), out_shape=(vmem((tokens,...  22.5 us
    unnamed x3, local copies, waits for them, and re-layouts  2.05 us

profile of v2, /device:TPU:0, one launch (start us, length us, event | category | flops | bytes accessed | tf_op | source)
XLA Modules:
  0.0 25.2 jit_solution(629995773400908054)
XLA Ops:
  0.6 22.5 %shard_map.94 = (bf16[256,1024]{1,0:T(8,128)(2,1)S(1)}, bf16[256,128]{1,0:T(8,128)(2,1)S(1)}, bf16[256,128]{1,0:T(8,128)(2,1)S(1)}) custom-call(bf16[256,1024]{1,0:T(8,128)(2,1)} %q_hbm.1, bf16[256,128]{1,0:T(8,128)(2,1)} %k_hbm.1, bf16[256,128]{1,0:T(8,128)(2,1)} %v_hbm.1, bf16[256,1024]{1,0:T(8,128)(2,1)} %o_hbm.1, bf16[64,4096]{1,0:T(8,128)(2,1)} %g_hbm.1, ...), custom_call_target="tpu_custom_call" | custom-call | tf_op jit(solution)/shard_map/pallas_call | solution.py:325
  23.1 0.8 %copy.13 = bf16[256,1024]{1,0:T(8,128)(2,1)} copy(bf16[256,1024]{1,0:T(8,128)(2,1)S(1)} %get-tuple-element.3) | data formatting | bytes 1048576
  23.9 0.6 %copy.14 = bf16[256,128]{1,0:T(8,128)(2,1)} copy(bf16[256,128]{1,0:T(8,128)(2,1)S(1)} %get-tuple-element.4) | data formatting | bytes 131072
  24.5 0.6 %copy.15 = bf16[256,128]{1,0:T(8,128)(2,1)} copy(bf16[256,128]{1,0:T(8,128)(2,1)S(1)} %get-tuple-element.5) | data formatting | bytes 131072

commit v3 on v2

--- a/solution.py
+++ b/solution.py
@@ -232,6 +232,14 @@
         span_probs(1, 1, False)
 
     steps = (0,) + ((1, 2, 3) if tp == 4 else tuple(range(1, tp)))
+    def own_terms(s):
+        total = dq_acc[s] + chunk_terms(0, 0, s)
+        if n == 2:
+            finish_query(s, total)
+        else:
+            dq_acc[s] = total
+
+    late = []
     for i, k in enumerate(steps):
         if k == 0:
             s = me
@@ -260,11 +268,13 @@
                 send_key_partial(1)
                 dq_acc[s] += dot(dscore, kb[1])
 
-        total = dq_acc[s] + chunk_terms(0, 0, s)
-        if n == 2:
-            finish_query(s, total)
+        if i < tp - 2:
+            own_terms(s)
         else:
-            dq_acc[s] = total
+            late.append(s)
+
+    for s in late:
+        own_terms(s)
 
     if n > 2:
 

time: 25.3 us -> 24.5 us (0.968)
  Pallas kernels: 22.5 us -> 21.7 us
    pallas_call x1, Pallas kernels: 22.5 us -> 21.7 us  [local(): pl.pallas_call(functools.partial(kernel, n, tp), out_shape=(vmem((tokens,...]
where the time goes in v3:
time: 24.5 us; the launch traced here: 24.4 us
  Pallas kernels  21.7 us (89%)
  local copies, waits for them, and re-layouts  2.05 us (8%)
  between operations  0.64 us (3%)
    pallas_call x1, Pallas kernels, local(): pl.pallas_call(functools.partial(kernel, n, tp), out_shape=(vmem((tokens,...  21.7 us
    unnamed x3, local copies, waits for them, and re-layouts  2.05 us

profile of v3, /device:TPU:0, one launch (start us, length us, event | category | flops | bytes accessed | tf_op | source)
XLA Modules:
  0.0 24.4 jit_solution(8146186330100865313)
XLA Ops:
  0.6 21.7 %shard_map.94 = (bf16[256,1024]{1,0:T(8,128)(2,1)S(1)}, bf16[256,128]{1,0:T(8,128)(2,1)S(1)}, bf16[256,128]{1,0:T(8,128)(2,1)S(1)}) custom-call(bf16[256,1024]{1,0:T(8,128)(2,1)} %q_hbm.1, bf16[256,128]{1,0:T(8,128)(2,1)} %k_hbm.1, bf16[256,128]{1,0:T(8,128)(2,1)} %v_hbm.1, bf16[256,1024]{1,0:T(8,128)(2,1)} %o_hbm.1, bf16[64,4096]{1,0:T(8,128)(2,1)} %g_hbm.1, ...), custom_call_target="tpu_custom_call" | custom-call | tf_op jit(solution)/shard_map/pallas_call | solution.py:335
  22.3 0.8 %copy.13 = bf16[256,1024]{1,0:T(8,128)(2,1)} copy(bf16[256,1024]{1,0:T(8,128)(2,1)S(1)} %get-tuple-element.3) | data formatting | bytes 1048576
  23.1 0.6 %copy.14 = bf16[256,128]{1,0:T(8,128)(2,1)} copy(bf16[256,128]{1,0:T(8,128)(2,1)S(1)} %get-tuple-element.4) | data formatting | bytes 131072
  23.8 0.6 %copy.15 = bf16[256,128]{1,0:T(8,128)(2,1)} copy(bf16[256,128]{1,0:T(8,128)(2,1)S(1)} %get-tuple-element.5) | data formatting | bytes 131072
